TPU v7x, 32 devices: a whole 2x2x4 slice. The times are simulated.
32 devices in a mesh: tile: 8 (over y, x, core), corner: 4 (over z).
Axes of the slice: x: 2, y: 2, z: 4, core: 2. Of those that a mesh axis runs over, the one named last changes fastest.
Arguments:
- mask: float32 [1024, 384], P('tile'), may hold values from 0 to 1
- target: int32 [1024, 384], P('tile'), may hold values 0 or 1
- pixel_weight: float32 [1024, 384], P('tile'), may hold values from 0.49 to 108
- row_taps: float32 [4, 8, 2, 129], replicated, may hold values from -2 to 2
- col_taps: float32 [4, 8, 2, 129], replicated, may hold values from -2 to 2
- kernel_weights: float32 [4, 8], replicated, may hold values from 0.03 to 0.25
- corner_set: int32 [16], P('corner'), may hold values from 0 to 3
- dose: float32 [16], P('corner'), may hold values from 0.8 to 1.25
Outputs:
- soft_error: float32 [1024, 384], P('tile')
- new_mask: float32 [1024, 384], P(('tile', 'corner'))
Inputs may be any that keep to these rules, and one draw needn't show every extreme that they name: `corner_set`: each corner names one of 4 focus settings. target pixels are 0 or 1.
All inputs are finite; a program needn't handle non-finite values. No bound on the sum of `target` on one device may be relied on, other than what follows from the above.
Results may differ from a plain program's by a relative error of at most 0.0051.
Values may be sent and summed in bfloat16 or wider, within the bound.
A program may use at most 64 MiB of HBM per device.

v0:
```python
import jax
import jax.numpy as jnp
from jax import lax
from jax.sharding import PartitionSpec as P

block_cols = 128
lse_sharp = 6.0
print_steep = 3.0
print_level = 1.0
step_rate = 0.25
small_eps = 1e-06


def with_halo(value, sides, width):
    for axis, dim in sides:
        count, length = (lax.axis_size(axis), value.shape[dim])
        up = [(i, (i + 1) % count) for i in range(count - 1)]
        down = [(j, i) for i, j in up]
        last = lax.slice_in_dim(value, length - width, length, axis=dim)
        leading = lax.slice_in_dim(value, 0, width, axis=dim)
        before = lax.ppermute(last, axis, up)
        after = lax.ppermute(leading, axis, down)
        value = jnp.concatenate([before, value, after], axis=dim)
    return value


def passed_along(value, axis, steps):
    count = lax.axis_size(axis)
    leading, last = (max(0, -steps), min(count, count - steps))
    return lax.ppermute(value, axis, [(source, source + steps) for source in range(leading, last)])


def toeplitz(tap_values, row_count):
    leading = tap_values.shape[:-1]
    span_width = row_count + tap_values.shape[-1] - 1
    padded = jnp.concatenate(
        [tap_values, jnp.zeros(leading + (row_count,), tap_values.dtype)], axis=-1
    )
    repeated = jnp.tile(padded, (1,) * len(leading) + (row_count,))
    return repeated[..., : row_count * span_width].reshape(leading + (row_count, span_width))


def column_filter(masked, band_matrix):
    reach_cols = (band_matrix.shape[-1] - block_cols) // 2
    col_count = masked.shape[1]
    padded = jnp.pad(masked, ((0, 0), (reach_cols, reach_cols)))
    windows = jnp.stack(
        [
            padded[:, b * block_cols : b * block_cols + block_cols + 2 * reach_cols]
            for b in range(col_count // block_cols)
        ],
        axis=0,
    )
    product = jnp.einsum("bri,poi->prbo", windows, band_matrix, preferred_element_type=jnp.float32)
    return product.reshape(2, masked.shape[0], col_count)


def row_filter(band_matrix, cfield):
    product = jnp.einsum("aij,bjx->abix", band_matrix, cfield, preferred_element_type=jnp.float32)
    return (product[0, 0] - product[1, 1], product[0, 1] + product[1, 0])


def row_adjoint(band_matrix, cotangent):
    product = jnp.einsum(
        "aij,bix->abjx", band_matrix, cotangent, preferred_element_type=jnp.float32
    )
    return jnp.stack([product[0, 0] + product[1, 1], product[0, 1] - product[1, 0]])


def column_adjoint(back_field, band_matrix):
    reach_cols = (band_matrix.shape[-1] - block_cols) // 2
    line_count = back_field.shape[1]
    col_count = back_field.shape[2]
    blocks = back_field.reshape(2, line_count, col_count // block_cols, block_cols)
    pieces = jnp.einsum("prbo,poi->bri", blocks, band_matrix, preferred_element_type=jnp.float32)
    summed = jnp.zeros((line_count, col_count + 2 * reach_cols), jnp.float32)
    for b in range(col_count // block_cols):
        summed = summed.at[:, b * block_cols : b * block_cols + block_cols + 2 * reach_cols].add(
            pieces[b]
        )
    return summed[:, reach_cols : reach_cols + col_count]


def local(mask, target, pixel_weight, row_taps, col_taps, kernel_weights, corner_set, dose):
    row_count, col_count = mask.shape
    reach_rows = (row_taps.shape[-1] - 1) // 2
    set_count = row_taps.shape[0]
    masked = mask.astype(jnp.bfloat16)
    extended = with_halo(masked, (("tile", 0),), reach_rows)
    target_value = target.astype(jnp.float32)
    exp_total = jnp.zeros((row_count, col_count), jnp.float32)
    corner_states = []
    for c in range(corner_set.shape[0]):
        chosen = (jnp.arange(set_count, dtype=jnp.int32) == corner_set[c]).astype(jnp.float32)
        row_values = jnp.sum(chosen[:, None, None, None] * row_taps, axis=0)
        col_values = jnp.sum(chosen[:, None, None, None] * col_taps, axis=0)
        weights = jnp.sum(chosen[:, None] * kernel_weights, axis=0)
        row_bands = toeplitz(row_values.astype(jnp.bfloat16), row_count)
        col_bands = toeplitz(col_values.astype(jnp.bfloat16), block_cols)

        def forward(running, inputs):
            row_band, col_band, kernel_weight = inputs
            cfield = column_filter(extended, col_band).astype(jnp.bfloat16)
            field_real, field_imag = row_filter(row_band, cfield)
            running = running + kernel_weight * (field_real * field_real + field_imag * field_imag)
            return (running, jnp.stack([field_real, field_imag]).astype(jnp.bfloat16))

        summed, fields = lax.scan(
            forward, jnp.zeros((row_count, col_count), jnp.float32), (row_bands, col_bands, weights)
        )
        intensity = dose[c] * summed
        printed = jax.nn.sigmoid(print_steep * (intensity - print_level))
        differ = printed - target_value
        exp_error = jnp.exp(lse_sharp * (differ * differ))
        exp_total = exp_total + exp_error
        corner_states.append((row_bands, col_bands, weights, fields, printed, exp_error, dose[c]))
    denominator = lax.psum(exp_total.astype(jnp.bfloat16), "corner").astype(jnp.float32)
    soft_error = jnp.log(denominator) / lse_sharp
    grad_ext = jnp.zeros((row_count + 2 * reach_rows, col_count), jnp.float32)
    for corner_state in corner_states:
        row_bands, col_bands, weights, fields, printed, exp_error, corner_dose = corner_state
        slope = (
            pixel_weight
            * (exp_error / denominator)
            * (2.0 * (printed - target_value))
            * printed
            * (1.0 - printed)
            * print_steep
        )
        factor = 2.0 * corner_dose * slope

        def backward(running, inputs):
            row_band, col_band, kernel_weight, field_pair = inputs
            cotangent = (factor * kernel_weight * field_pair).astype(jnp.bfloat16)
            back_field = row_adjoint(row_band, cotangent).astype(jnp.bfloat16)
            return (running + column_adjoint(back_field, col_band), None)

        grad_ext, _ = lax.scan(backward, grad_ext, (row_bands, col_bands, weights, fields))
    upper_rim = grad_ext[:reach_rows]
    lower_rim = grad_ext[row_count + reach_rows :]
    middle = grad_ext[reach_rows : row_count + reach_rows]
    from_below = passed_along(upper_rim, "tile", -1)
    from_above = passed_along(lower_rim, "tile", 1)
    gradient = (
        middle
        + jnp.pad(from_above, ((0, row_count - reach_rows), (0, 0)))
        + jnp.pad(from_below, ((row_count - reach_rows, 0), (0, 0)))
    )
    share_rows = row_count // lax.axis_size("corner")
    first_row = lax.axis_index("corner") * share_rows
    own_mask = lax.dynamic_slice_in_dim(mask, first_row, share_rows, 0)
    pixel_count = row_count * lax.axis_size("tile") * col_count
    summed_grad = lax.psum(gradient, "corner")
    square = lax.psum(jnp.sum(summed_grad * summed_grad), "tile")
    own_rows = lax.dynamic_slice_in_dim(summed_grad, first_row, share_rows, 0)
    root_mean = jnp.sqrt(square / pixel_count + small_eps)
    new_mask = jnp.clip(own_mask - step_rate / root_mean * own_rows, 0.0, 1.0)
    return (soft_error, new_mask)


def solution(mesh):
    placed = (
        P("tile", None),
        P("tile", None),
        P("tile", None),
        P(),
        P(),
        P(),
        P("corner"),
        P("corner"),
    )
    return jax.shard_map(
        local,
        mesh=mesh,
        in_specs=placed,
        out_specs=(P("tile", None), P(("tile", "corner"), None)),
        check_vma=False,
    )
```

profile of v0, /device:TPU:0, one launch (start us, length us, event | category | flops | bytes accessed | tf_op | source)
XLA Modules:
  0.0 593.3 jit_solution(7374306210661256130)
XLA Ops:
  9.4 3.0 collective-permute-start
  27.0 3.1 tile.87
  32.7 3.1 tile.37
  38.4 3.1 tile.39
  44.2 3.1 tile.81
  50.8 3.1 tile.83
  56.5 3.1 tile.33
  62.1 3.1 tile.35
  68.8 49.2 %while.135 = (s32[]{:T(128)}, f32[128,384]{0,1:T(8,128)}, bf16[8,2,128,384]{2,3,0,1:T(8,128)(2,1)}, f32[8]{0:T(128)S(1)}, bf16[8,2,128,256]{3,2,1,0:T(8,128)(2,1...) while((s32[]{:T(128)}, f32[128,384]{0,1:T(8,128)}, ...), condition=%wide.region_19.20_spmd.clone, body=%wide.region_18.19_spmd.clone.sunk | while | flops 203685888 | bytes 5506679 | solution.py:108
  78.1 2.3 bitcast_add_fusion.11
  84.4 2.3 bitcast_add_fusion.11
  90.6 2.3 bitcast_add_fusion.11
  96.9 2.3 bitcast_add_fusion.11
  103.1 2.3 bitcast_add_fusion.11
  109.4 2.3 bitcast_add_fusion.11
  115.6 2.3 bitcast_add_fusion.11
  121.2 49.1 %while.133 = (s32[]{:T(128)}, f32[128,384]{0,1:T(8,128)}, bf16[8,2,128,384]{2,3,0,1:T(8,128)(2,1)}, f32[8]{0:T(128)S(1)}, bf16[8,2,128,256]{3,2,1,0:T(8,128)(2,1...) while((s32[]{:T(128)}, f32[128,384]{0,1:T(8,128)}, ...), condition=%wide.region_9.10_spmd.clone, body=%wide.region_8.9_spmd.clone.sunk | while | flops 203685888 | bytes 5506679 | solution.py:108
  130.5 2.3 bitcast_add_fusion.9
  136.7 2.3 bitcast_add_fusion.9
  143.0 2.3 bitcast_add_fusion.9
  173.5 38.1 %while.134 = (s32[]{:T(128)}, f32[128,384]{0,1:T(8,128)S(1)}, bf16[8,2,128,384]{2,3,0,1:T(8,128)(2,1)}, f32[8]{0:T(128)S(1)}, bf16[8,2,128,256]{3,2,1,0:T(8,128)...) while((s32[]{:T(128)}, f32[128,384]{0,1:T(8,128)S(1)}, ...), condition=%wide.region_14.15_spmd.clone, body=%wide.region_13.14_spmd.clone.sunk | while | flops 203685888 | bytes 5506679 | solution.py:108
  213.8 38.2 %while.132 = (s32[]{:T(128)}, f32[128,384]{0,1:T(8,128)S(1)}, bf16[8,2,128,384]{2,3,0,1:T(8,128)(2,1)}, f32[8]{0:T(128)S(1)}, bf16[8,2,128,256]{3,2,0,1:T(8,128)...) while((s32[]{:T(128)}, f32[128,384]{0,1:T(8,128)S(1)}, ...), condition=%wide.region_4.5_spmd.clone, body=%wide.region_3.4_spmd.clone.sunk | while | flops 203685888 | bytes 5506679 | solution.py:108
  252.1 4.9 add_convert_fusion
  265.0 30.6 %all-reduce.21.cloned.1.call-done = bf16[128,384]{1,0:T(8,128)(2,1)} async-done(((bf16[128,384]{1,0:T(8,128)(2,1)}), bf16[128,384]{1,0:T(8,128)(2,1)}) %all-reduce.21.cloned.1.call-update) | async-done | bytes 98320 | tf_op jit(solution)/shard_map/psum | solution.py:117
  295.5 5.0 fusion.160
  300.6 58.7 %while.136 = (s32[]{:T(128)}, f32[256,384]{0,1:T(8,128)S(1)}, bf16[8,2,128,256]{3,2,0,1:T(8,128)(2,1)}, f32[8]{0:T(128)S(1)}, f32[128,384]{0,1:T(8,128)S(1)}, /*...) while((s32[]{:T(128)}, f32[256,384]{0,1:T(8,128)S(1)}, ...), condition=%wide.region_25.26_spmd.clone, body=%wide.region_23.25_spmd.clone.sunk | while | flops 203374592 | bytes 10618519 | solution.py:138
  360.4 56.3 %while.129 = (s32[]{:T(128)}, f32[256,384]{0,1:T(8,128)S(1)}, bf16[8,2,128,256]{2,3,1,0:T(8,128)(2,1)}, f32[8]{0:T(128)S(1)}, f32[128,384]{0,1:T(8,128)S(1)}, /*...) while((s32[]{:T(128)}, f32[256,384]{0,1:T(8,128)S(1)}, ...), condition=%wide.region_28.29_spmd, body=%wide.region_26.28_spmd.sunk | while | flops 203276288 | bytes 10618501 | solution.py:138
  417.8 57.5 %while.130 = (s32[]{:T(128)}, f32[256,384]{0,1:T(8,128)S(1)}, bf16[8,2,128,256]{2,3,1,0:T(8,128)(2,1)}, f32[8]{0:T(128)S(1)}, f32[128,384]{0,1:T(8,128)S(1)}, /*...) while((s32[]{:T(128)}, f32[256,384]{0,1:T(8,128)S(1)}, ...), condition=%wide.region_31.32_spmd, body=%wide.region_29.31_spmd.sunk | while | flops 203276288 | bytes 10618501 | solution.py:138
  475.4 50.3 %while.131 = (s32[]{:T(128)}, f32[256,384]{0,1:T(8,128)S(1)}, bf16[8,2,128,256]{2,3,1,0:T(8,128)(2,1)S(1)}, f32[8]{0:T(128)S(1)}, f32[128,384]{0,1:T(8,128)S(1)}...) while((s32[]{:T(128)}, f32[256,384]{0,1:T(8,128)S(1)}, ...), condition=%wide.region_34.35_spmd, body=%wide.region_32.34_spmd.sunk | while | flops 203276288 | bytes 10617993 | solution.py:138
  528.5 3.5 collective-permute-done.3
  532.7 37.5 %all-reduce.23.cloned.1.call-done = f32[128,384]{1,0:T(8,128)} async-done(((f32[128,384]{1,0:T(8,128)}), f32[128,384]{1,0:T(8,128)}) %all-reduce.23.cloned.1.call-update) | async-done | bytes 196624 | tf_op jit(solution)/shard_map/psum | solution.py:153
  571.8 12.4 %psum.23 = f32[]{:T(128)} all-reduce(f32[]{:T(128)} %multiply_reduce_fusion), channel_id=1, replica_groups=mesh['tile'=8,'corner'=4] {'tile'}, use_global_device_ids=true, to_apply=%region_37.38 | all-reduce | flops 1 | bytes 8 | tf_op jit(solution)/shard_map/psum | solution.py:154
  (750 shorter events, 430.4 us)
Async XLA Ops:
  7.2 288.4 %all-reduce.21.cloned.1.call-start = ((), (), s32[]{:S(2)}) async-start(), calls=%async_computation | async-start | bytes 196608 | tf_op jit(solution)/shard_map/psum | solution.py:117
  8.2 0.6 copy-start.7
  9.4 57.1 %collective-permute-start = (bf16[64,384]{1,0:T(8,128)(2,1)}, bf16[64,384]{1,0:T(8,128)(2,1)}, u32[]{:S(2)}, u32[]{:S(2)}) collective-permute-start(bf16[64,384]{1,0:T(8,128)(2,1)} %get-tuple-element.1630), channel_id=1, source_target_pairs={{0,4},{4,8},{8,12},{12,16},{16,20},{20,24},{24,28},{1,5},{5,9},{9,... | collective-permute-start | bytes 147464 | tf_op jit(solution)/shard_map/ppermute | solution.py:21
  12.4 54.1 %collective-permute-start.1 = (bf16[64,384]{1,0:T(8,128)(2,1)}, bf16[64,384]{1,0:T(8,128)(2,1)}, u32[]{:S(2)}, u32[]{:S(2)}) collective-permute-start(bf16[64,384]{1,0:T(8,128)(2,1)} %get-tuple-element.1631), channel_id=1, source_target_pairs={{4,0},{8,4},{12,8},{16,12},{20,16},{24,20},{28,24},{5,1},{9,5},{13... | collective-permute-start | bytes 147464 | tf_op jit(solution)/shard_map/ppermute | solution.py:22
  30.1 1.2 copy-start.13
  35.9 1.2 copy-start.12
  41.5 1.3 copy-start.11
  47.3 1.0 copy-start
  48.3 1.2 copy-start.10
  53.9 1.2 copy-start.9
  65.3 1.2 copy-start.8
  118.0 3.2 copy-start.15
  170.3 3.2 copy-start.14
  211.5 2.3 copy-start.16
  252.1 7.0 %copy-start.5 = (f32[128,384]{1,0:T(8,128)}, f32[128,384]{1,0:T(8,128)S(1)}, u32[]{:S(2)}) copy-start(f32[128,384]{1,0:T(8,128)S(1)} %copy.88) | copy-start | bytes 589828
  252.1 9.4 %copy-start.1 = (bf16[8,2,32768]{2,0,1:T(8,128)(2,1)S(1)}, bf16[8,2,32768]{2,0,1:T(8,128)(2,1)}, u32[]{:S(2)}) copy-start(bf16[8,2,32768]{2,0,1:T(8,128)(2,1)} %copy-done) | copy-start | bytes 3145732
  257.1 313.2 %all-reduce.23.cloned.1.call-start = ((), (), s32[]{:S(2)}) async-start(), calls=%async_computation.1 | async-start | bytes 393216 | tf_op jit(solution)/shard_map/psum | solution.py:153
  263.2 32.3 %copy-start.2 = (f32[128,384]{1,0:T(8,128)S(1)}, f32[128,384]{1,0:T(8,128)}, u32[]{:S(2)}) copy-start(f32[128,384]{1,0:T(8,128)} %copy.103) | copy-start | bytes 589828
  263.2 32.3 %copy-start.3 = (f32[128,384]{1,0:T(8,128)S(1)}, f32[128,384]{1,0:T(8,128)}, u32[]{:S(2)}) copy-start(f32[128,384]{1,0:T(8,128)} %copy.93) | copy-start | bytes 589828
  263.2 32.3 %copy-start.4 = (f32[128,384]{1,0:T(8,128)S(1)}, f32[128,384]{1,0:T(8,128)}, u32[]{:S(2)}) copy-start(f32[128,384]{1,0:T(8,128)} %copy.98) | copy-start | bytes 589828
  263.2 32.3 %copy-start.6 = (f32[128,384]{1,0:T(8,128)S(1)}, f32[128,384]{1,0:T(8,128)}, u32[]{:S(2)}) copy-start(f32[128,384]{1,0:T(8,128)} %copy-done.5) | copy-start | bytes 589828
  525.9 2.6 collective-permute-start.2
  527.2 4.8 collective-permute-start.3
Sparse Core Ops, SparseCore 0:
  257.2 38.2 all-reduce.20
  532.9 37.3 all-reduce.22
where the time goes:
time: 598 us; the launch traced here: 593 us
  other arithmetic  208 us (35%)
  matrix products  152 us (25%)
  local copies, waits for them, and re-layouts  121 us (20%)
  waiting for transfers between devices  71.6 us (12%)
  between operations  17.8 us (3%)
  blocking collectives  12.4 us (2%)
  starting transfers between devices  6.91 us (1%)
    add x32, other arithmetic, forward(): running + kernel_weight * (field_real * field_real + field_imag * field_i...  48.1 us
    scatter-add x64, other arithmetic, column_adjoint(): summed.at[:, b * block_cols:b * block_cols + block_cols + 2 * reach_cols]  47.9 us
    another operation x129, other arithmetic  45.9 us
    dot_general x32, matrix products, row_adjoint(): jnp.einsum('aij,bix->abjx', band_matrix, cotangent, preferred_element_typ...  43.4 us
    dot_general x32, matrix products, column_filter(): jnp.einsum('bri,poi->prbo', windows, band_matrix, preferred_element_type=...  38.8 us
    dot_general x32, matrix products, row_filter(): jnp.einsum('aij,bjx->abix', band_matrix, cfield, preferred_element_type=j...  38.4 us
    dynamic_slice x64, local copies, waits for them, and re-layouts, local(): lax.scan(forward, jnp.zeros((row_count, col_count), jnp.float32), (row_ba...  38.3 us
    psum x1, waiting for transfers between devices, local(): summed_grad = lax.psum(gradient, 'corner')  37.5 us
  transfers between devices with their start and end apart: 6, of which 3 were waited for; matrix products, arithmetic and copies ran while one was open for 10% of the time, Pallas kernels for 0%

commit v1 on v0

v1 whole, which is shorter than its diff:
```python
import functools
import jax
import jax.numpy as jnp
from jax import lax
from jax.experimental import pallas as pl
from jax.experimental.pallas import tpu as pltpu
from jax.sharding import PartitionSpec as P

lse_sharp = 6.0
print_steep = 3.0
print_level = 1.0
step_rate = 0.25
small_eps = 1e-06
BLK = 128
F32 = jnp.float32
BF16 = jnp.bfloat16
MESH = pl.DeviceIdType.MESH


def kernel(
    n_t, n_c, mask_ref, target_ref, weight_ref, rt_ref, ct_ref, kw_ref, cs_ref, dose_ref,
    soft_ref, new_ref,
    xp, xw, tb, ra, cb, cf, fields, ssc, ssend, srecv, infosend, inforecv, fsend, frecv,
    softsend, softrecv, bkr, bkm, rimsend, rimrecv, gown, gsend, grecv, sqsend, sqrecv,
    sqtsend, sqtrecv,
    halo_s, halo_r, info_s, info_r, s_s, s_r, f_s, f_r, soft_s, soft_r, rim_s, rim_r,
    g_s, g_r, sq_s, sq_r, sqt_s, sqt_r,
):
    t = lax.axis_index("tile")
    z = lax.axis_index("corner")
    rows, cols = mask_ref.shape
    n_sets, n_k = kw_ref.shape
    taps = rt_ref.shape[-1]
    reach = (taps - 1) // 2
    ext = rows + 2 * reach
    win = BLK + 2 * reach
    n_b = cols // BLK
    share = rows // n_c
    per = n_sets * n_k // n_c
    local_corners = cs_ref.shape[0]
    s_me = (z * per) // n_k
    k_me = (z * per) % n_k

    def zpeer(d):
        return lax.rem(z + d, n_c)

    def tpeer(d):
        return lax.rem(t + d, n_t)

    def remote(src, dst, ssem, rsem, dev):
        return pltpu.make_async_remote_copy(
            src_ref=src, dst_ref=dst, send_sem=ssem, recv_sem=rsem,
            device_id=dev, device_id_type=MESH,
        )

    barrier = pltpu.get_barrier_semaphore()
    for d in range(1, n_c):
        pl.semaphore_signal(barrier, inc=1, device_id=(t, zpeer(d)), device_id_type=MESH)
    for d in range(1, n_t):
        pl.semaphore_signal(barrier, inc=1, device_id=(tpeer(d), z), device_id_type=MESH)

    padded = jnp.concatenate([mask_ref[...], jnp.zeros((rows, 2 * reach), F32)], axis=1)
    padded = pltpu.roll(padded, reach, 1)
    xp[reach : reach + rows, :] = padded.astype(BF16)

    @pl.when(t == 0)
    def _():
        xp[0:reach, :] = jnp.zeros((reach, cols + 2 * reach), BF16)
        rimrecv[1] = jnp.zeros((reach, cols), BF16)

    @pl.when(t == n_t - 1)
    def _():
        xp[reach + rows : ext, :] = jnp.zeros((reach, cols + 2 * reach), BF16)
        rimrecv[0] = jnp.zeros((reach, cols), BF16)

    for i in range(local_corners):
        infosend[2 * i : 2 * i + 1, :] = jnp.full((1, cols), cs_ref[i].astype(F32), F32)
        infosend[2 * i + 1 : 2 * i + 2, :] = jnp.full((1, cols), dose_ref[i], F32)
    inforecv[z] = infosend[...]

    pl.semaphore_wait(barrier, n_c - 1 + n_t - 1)

    down = remote(xp.at[pl.ds(rows, reach)], xp.at[pl.ds(0, reach)],
                  halo_s.at[0], halo_r.at[0], (tpeer(1), z))
    up = remote(xp.at[pl.ds(reach, reach)], xp.at[pl.ds(reach + rows, reach)],
                halo_s.at[1], halo_r.at[1], (tpeer(n_t - 1), z))

    @pl.when(t < n_t - 1)
    def _():
        down.start()

    @pl.when(t > 0)
    def _():
        up.start()

    infos = [
        remote(infosend, inforecv.at[z], info_s.at[d - 1], info_r.at[d - 1], (t, zpeer(d)))
        for d in range(1, n_c)
    ]
    for copy in infos:
        copy.start()

    tb[...] = jnp.zeros(tb.shape, F32)

    def tables(k, _):
        for p in range(2):
            tb[p : p + 1, 0:taps] = rt_ref[s_me, k_me + k, p : p + 1, :].astype(BF16).astype(F32)
            tb[2 + p : 3 + p, 0:taps] = ct_ref[s_me, k_me + k, p : p + 1, :].astype(BF16).astype(F32)

        def band(row, length, width):
            wide = jnp.broadcast_to(tb[row : row + 1, 0:width], (length, width))
            return pltpu.roll(wide, 0, 1, stride=1, stride_axis=0)

        re = band(0, rows, ext)
        im = band(1, rows, ext)
        ra[k, 0:rows, 0:ext] = re.astype(BF16)
        ra[k, rows : 2 * rows, ext : 2 * ext] = re.astype(BF16)
        ra[k, 0:rows, ext : 2 * ext] = (-im).astype(BF16)
        ra[k, rows : 2 * rows, 0:ext] = im.astype(BF16)
        base = pl.multiple_of(k * 2 * BLK, 2 * BLK)
        cb[pl.ds(base, BLK), :] = band(2, BLK, win).astype(BF16)
        cb[pl.ds(base + BLK, BLK), :] = band(3, BLK, win).astype(BF16)
        return 0

    lax.fori_loop(0, per, tables, 0)

    @pl.when(t > 0)
    def _():
        down.wait_recv()

    @pl.when(t < n_t - 1)
    def _():
        up.wait_recv()

    for b in range(n_b):
        xw[b * ext : (b + 1) * ext, :] = xp[:, b * BLK : b * BLK + win]
    ssc[...] = jnp.zeros(ssc.shape, F32)

    def forward(k, _):
        base = pl.multiple_of(k * 2 * BLK, 2 * BLK)
        c = lax.dot_general(
            xw[...], cb[pl.ds(base, 2 * BLK), :], (((1,), (1,)), ((), ())),
            preferred_element_type=F32,
        ).astype(BF16)
        for b in range(n_b):
            for p in range(2):
                cf[p * ext : (p + 1) * ext, b * BLK : (b + 1) * BLK] = c[
                    b * ext : (b + 1) * ext, p * BLK : (p + 1) * BLK
                ]
        field = jnp.dot(ra[k], cf[...], preferred_element_type=F32)
        re = field[0:rows]
        im = field[rows : 2 * rows]
        power = kw_ref[s_me, k_me + k] * (re * re + im * im)
        ssc[...] += power.reshape(ssc.shape)
        fields[k] = field.astype(BF16)
        return 0

    lax.fori_loop(0, per, forward, 0)

    ssend[...] = ssc[...].astype(BF16)
    scopies = [
        remote(ssend.at[zpeer(d)], srecv.at[z], s_s.at[d - 1], s_r.at[d - 1], (t, zpeer(d)))
        for d in range(1, n_c)
    ]
    for copy in scopies:
        copy.start()
    srecv[z] = ssend[z]
    for copy in infos:
        copy.wait_recv()
    for copy in scopies:
        copy.wait_recv()

    row0 = pl.multiple_of(z * share, share)
    owners = n_c // n_sets
    step = 16

    def pixels(j, _):
        r = pl.multiple_of(j * step, step)
        sums = []
        for s in range(n_sets):
            total = srecv[s * owners, pl.ds(r, step), :].astype(F32)
            for o in range(1, owners):
                total = total + srecv[s * owners + o, pl.ds(r, step), :].astype(F32)
            sums.append(total)
        goal = target_ref[pl.ds(row0 + r, step), :].astype(F32)
        pixel = weight_ref[pl.ds(row0 + r, step), :]
        for b in range(n_b):
            cut = slice(b * BLK, (b + 1) * BLK)
            den = jnp.zeros((step, BLK), F32)
            acc = [jnp.zeros((step, BLK), F32) for _ in range(n_sets)]
            tv = goal[:, cut]
            for c in range(n_c * local_corners):
                zc, i = divmod(c, local_corners)
                which = inforecv[zc, 2 * i : 2 * i + 1, cut]
                amount = inforecv[zc, 2 * i + 1 : 2 * i + 2, cut]
                which = jnp.broadcast_to(which, (step, BLK))
                chosen = sums[n_sets - 1][:, cut]
                for s in range(n_sets - 1):
                    chosen = jnp.where(which == float(s), sums[s][:, cut], chosen)
                printed = 1.0 / (1.0 + jnp.exp(print_steep * (print_level - amount * chosen)))
                differ = printed - tv
                err = jnp.exp(lse_sharp * (differ * differ))
                den = den + err
                part = amount * err * differ * (printed * (1.0 - printed))
                for s in range(n_sets):
                    acc[s] = acc[s] + jnp.where(which == float(s), part, 0.0)
            softsend[pl.ds(r, step), cut] = jnp.log(den) / lse_sharp
            scale = (4.0 * print_steep) * pixel[:, cut] / den
            for s in range(n_sets):
                fsend[s, pl.ds(r, step), cut] = (scale * acc[s]).astype(BF16)
        return 0

    lax.fori_loop(0, share // step, pixels, 0)

    fcopies = [
        remote(fsend.at[(zpeer(d) * per) // n_k], frecv.at[z], f_s.at[d - 1], f_r.at[d - 1],
               (t, zpeer(d)))
        for d in range(1, n_c)
    ]
    for copy in fcopies:
        copy.start()
    softs = [
        remote(softsend, softrecv.at[z], soft_s.at[d - 1], soft_r.at[d - 1], (t, zpeer(d)))
        for d in range(1, n_c)
    ]
    for copy in softs:
        copy.start()
    frecv[z] = fsend[s_me]
    softrecv[z] = softsend[...]
    for copy in fcopies:
        copy.wait_recv()

    def backward(k, _):
        factor = frecv[...].reshape(rows, cols).astype(F32) * kw_ref[s_me, k_me + k]
        both = jnp.concatenate([factor, factor], axis=0)
        cot = (both * fields[k].astype(F32)).astype(BF16)
        back = lax.dot_general(
            ra[k], cot, (((0,), (0,)), ((), ())), preferred_element_type=F32
        ).astype(BF16)
        for b in range(n_b):
            for p in range(2):
                piece = back[p * ext : (p + 1) * ext, b * BLK : (b + 1) * BLK]
                at = pl.ds(pl.multiple_of(k * 2 * BLK + p * BLK, BLK), BLK)
                low = b * 2 * reach
                bkr[low : low + reach, at] = piece[0:reach]
                bkr[low + reach : low + 2 * reach, at] = piece[reach + rows : ext]
                bkm[b * rows : (b + 1) * rows, at] = piece[reach : reach + rows]
        return 0

    lax.fori_loop(0, per, backward, 0)

    def column_sum(ref, count):
        g = jnp.dot(ref[...], cb[...], preferred_element_type=F32)
        strips = []
        for j in range(n_b + 1):
            value = None
            if j < n_b:
                value = g[j * count : (j + 1) * count, 0:BLK]
            if j > 0:
                other = g[(j - 1) * count : j * count, BLK : 2 * BLK]
                value = other if value is None else value + other
            strips.append(value)
        wide = jnp.concatenate(strips, axis=1)
        return pltpu.roll(wide, cols + reach, 1)[:, 0:cols]

    rim = column_sum(bkr, 2 * reach)
    rimsend[...] = rim.astype(BF16).reshape(rimsend.shape)
    rim_up = remote(rimsend.at[0], rimrecv.at[0], rim_s.at[0], rim_r.at[0], (tpeer(n_t - 1), z))
    rim_down = remote(rimsend.at[1], rimrecv.at[1], rim_s.at[1], rim_r.at[1], (tpeer(1), z))

    @pl.when(t > 0)
    def _():
        rim_up.start()

    @pl.when(t < n_t - 1)
    def _():
        rim_down.start()

    middle = column_sum(bkm, rows)

    @pl.when(t < n_t - 1)
    def _():
        rim_up.wait_recv()

    @pl.when(t > 0)
    def _():
        rim_down.wait_recv()

    rims = jnp.concatenate([rimrecv[1], rimrecv[0]], axis=0).astype(F32)
    if rows > 2 * reach:
        gap = jnp.zeros((rows - 2 * reach, cols), F32)
        rims = jnp.concatenate([rims[0:reach], gap, rims[reach:]], axis=0)
    gown[...] = (middle + rims).reshape(gown.shape)
    gsend[...] = gown[...].astype(BF16)
    gcopies = [
        remote(gsend.at[zpeer(d)], grecv.at[d - 1], g_s.at[d - 1], g_r.at[d - 1], (t, zpeer(d)))
        for d in range(1, n_c)
    ]
    for copy in gcopies:
        copy.start()
    for copy in softs:
        copy.wait_recv()
    soft_ref[...] = softrecv[...].reshape(rows, cols)
    grad = gown[z]
    for d in range(1, n_c):
        gcopies[d - 1].wait_recv()
        grad = grad + grecv[d - 1].astype(F32)

    square = jnp.sum((grad * grad).reshape(share // 8, 8, cols), axis=0)
    part = square[:, 0:BLK]
    for b in range(1, n_b):
        part = part + square[:, b * BLK : (b + 1) * BLK]
    sqsend[...] = part
    sqz = [
        remote(sqsend, sqrecv.at[d - 1], sq_s.at[d - 1], sq_r.at[d - 1], (t, zpeer(d)))
        for d in range(1, n_c)
    ]
    for copy in sqz:
        copy.start()
    for d in range(1, n_c):
        sqz[d - 1].wait_recv()
        part = part + sqrecv[d - 1]
    sqtsend[...] = part
    sqt = [
        remote(sqtsend, sqtrecv.at[d - 1], sqt_s.at[d - 1], sqt_r.at[d - 1], (tpeer(d), z))
        for d in range(1, n_t)
    ]
    for copy in sqt:
        copy.start()
    for d in range(1, n_t):
        sqt[d - 1].wait_recv()
        part = part + sqtrecv[d - 1]
    total = jnp.sum(jnp.sum(part, axis=0, keepdims=True), axis=1, keepdims=True)
    rate = step_rate / jnp.sqrt(total / (rows * n_t * cols) + small_eps)
    own = mask_ref[pl.ds(row0, share), :]
    new_ref[...] = jnp.clip(own - rate * grad, 0.0, 1.0)

    @pl.when(t < n_t - 1)
    def _():
        down.wait_send()
        rim_down.wait_send()

    @pl.when(t > 0)
    def _():
        up.wait_send()
        rim_up.wait_send()

    for copy in infos + scopies + fcopies + softs + gcopies + sqz + sqt:
        copy.wait_send()


def solution(mesh):
    n_t, n_c = mesh.shape["tile"], mesh.shape["corner"]

    def local(mask, target, pixel_weight, row_taps, col_taps, kernel_weights, corner_set, dose):
        rows, cols = mask.shape
        n_sets, n_k, _, taps = row_taps.shape
        reach = (taps - 1) // 2
        ext, win, n_b = rows + 2 * reach, BLK + 2 * reach, cols // BLK
        share = rows // n_c
        per = n_sets * n_k // n_c
        info_rows = 8 * ((2 * corner_set.shape[0] + 7) // 8)
        vmem = pl.BlockSpec(memory_space=pltpu.VMEM)
        smem = pl.BlockSpec(memory_space=pltpu.SMEM)
        V = pltpu.VMEM
        dma = pltpu.SemaphoreType.DMA
        zc = dma((n_c - 1,))
        scratch = [
            V((ext, cols + 2 * reach), BF16),
            V((n_b * ext, win), BF16),
            V((8, max(ext, win)), F32),
            V((per, 2 * rows, 2 * ext), BF16),
            V((per * 2 * BLK, win), BF16),
            V((2 * ext, cols), BF16),
            V((per, 2 * rows, cols), BF16),
            V((n_c, share, cols), F32),
            V((n_c, share, cols), BF16),
            V((n_c, share, cols), BF16),
            V((info_rows, cols), F32),
            V((n_c, info_rows, cols), F32),
            V((n_sets, share, cols), BF16),
            V((n_c, share, cols), BF16),
            V((share, cols), F32),
            V((n_c, share, cols), F32),
            V((n_b * 2 * reach, per * 2 * BLK), BF16),
            V((n_b * rows, per * 2 * BLK), BF16),
            V((2, reach, cols), BF16),
            V((2, reach, cols), BF16),
            V((n_c, share, cols), F32),
            V((n_c, share, cols), BF16),
            V((n_c - 1, share, cols), BF16),
            V((8, BLK), F32),
            V((n_c - 1, 8, BLK), F32),
            V((8, BLK), F32),
            V((n_t - 1, 8, BLK), F32),
            dma((2,)), dma((2,)),
            zc, zc, zc, zc, zc, zc, zc, zc,
            dma((2,)), dma((2,)),
            zc, zc, zc, zc,
            dma((n_t - 1,)), dma((n_t - 1,)),
        ]
        return pl.pallas_call(
            functools.partial(kernel, n_t, n_c),
            out_shape=(
                jax.ShapeDtypeStruct((rows, cols), F32),
                jax.ShapeDtypeStruct((share, cols), F32),
            ),
            in_specs=[vmem] * 5 + [smem] * 3,
            out_specs=(vmem, vmem),
            scratch_shapes=scratch,
            compiler_params=pltpu.CompilerParams(
                collective_id=0, has_side_effects=True, vmem_limit_bytes=44 * 1024 * 1024
            ),
        )(mask, target, pixel_weight, row_taps, col_taps, kernel_weights, corner_set, dose)

    placed = (
        P("tile", None),
        P("tile", None),
        P("tile", None),
        P(),
        P(),
        P(),
        P("corner"),
        P("corner"),
    )
    return jax.shard_map(
        local,
        mesh=mesh,
        in_specs=placed,
        out_specs=(P("tile", None), P(("tile", "corner"), None)),
        check_vma=False,
    )
```

time: 598 us -> 51.7 us (0.09)
  other arithmetic: 208 us -> 0 us
  matrix products: 152 us -> 0 us
  local copies, waits for them, and re-layouts: 121 us -> 7.74 us
  waiting for transfers between devices: 71.6 us -> 0 us
  Pallas kernels: 0 us -> 43 us
  between operations: 17.8 us -> 0.66 us
  blocking collectives: 12.4 us -> 0 us
  starting transfers between devices: 6.91 us -> 0 us
    dot_general x128 -> x0, matrix products: 152 us -> none  [the longest x32 43.4 us: row_adjoint(): jnp.einsum('aij,bix->abjx', band_matrix, cotangent, preferred_element_typ...]
    psum x2 -> x0, waiting for transfers between devices: 68.1 us -> none  [the longest x1 37.5 us: local(): summed_grad = lax.psum(gradient, 'corner')]
    add x65 -> x0, other arithmetic: 51.7 us -> none  [the longest x32 48.1 us: forward(): running + kernel_weight * (field_real * field_real + field_imag * field_i...]
    scatter-add x64 -> x0, other arithmetic: 47.9 us -> none  [column_adjoint(): summed.at[:, b * block_cols:b * block_cols + block_cols + 2 * reach_cols]]
    another operation x129 -> x0, other arithmetic: 45.9 us -> none
    another operation x52 -> x0, local copies, waits for them, and re-layouts: 44 us -> none  [the longest x16 32.5 us: toeplitz(): repeated = jnp.tile(padded, (1,) * len(leading) + (row_count,))]
    pallas_call x0 -> x1, Pallas kernels: none -> 43 us  [local(): pl.pallas_call(functools.partial(kernel, n_t, n_c), out_shape=(jax.ShapeD...]
    dynamic_slice x64 -> x0, local copies, waits for them, and re-layouts: 38.3 us -> none  [local(): lax.scan(forward, jnp.zeros((row_count, col_count), jnp.float32), (row_ba...]
  transfers between devices with their start and end apart: 6 -> 0, of which waited for: 3 -> 0; matrix products, arithmetic and copies ran while one was open for 10% -> 0% of each run, Pallas kernels for 0% -> 0%
where the time goes in v1:
time: 51.7 us; the launch traced here: 51.4 us
  Pallas kernels  43 us (83%)
  local copies, waits for them, and re-layouts  7.74 us (15%)
  between operations  0.66 us (1%)
    pallas_call x1, Pallas kernels, local(): pl.pallas_call(functools.partial(kernel, n_t, n_c), out_shape=(jax.ShapeD...  43 us
    unnamed x18, local copies, waits for them, and re-layouts  7.74 us

profile of v1, /device:TPU:0, one launch (start us, length us, event | category | flops | bytes accessed | tf_op | source)
XLA Modules:
  0.0 51.4 jit_solution(170403583689992629)
XLA Ops:
  0.6 0.0 copy-start
  0.6 0.9 %copy-done = f32[128,384]{1,0:T(8,128)S(1)} copy-done((f32[128,384]{1,0:T(8,128)S(1)}, f32[128,384]{1,0:T(8,128)}, u32[]{:S(2)}) %copy-start) | copy-done | bytes 196632
  1.6 0.0 copy-start.1
  1.6 0.9 %copy-done.1 = s32[128,384]{1,0:T(8,128)S(1)} copy-done((s32[128,384]{1,0:T(8,128)S(1)}, s32[128,384]{1,0:T(8,128)}, u32[]{:S(2)}) %copy-start.1) | copy-done | bytes 196632
  2.5 0.0 copy-start.2
  2.5 0.9 %copy-done.2 = f32[128,384]{1,0:T(8,128)S(1)} copy-done((f32[128,384]{1,0:T(8,128)S(1)}, f32[128,384]{1,0:T(8,128)}, u32[]{:S(2)}) %copy-start.2) | copy-done | bytes 196632
  3.4 0.0 copy-start.3
  3.4 0.8 %copy-done.3 = f32[4,8,2,129]{3,2,1,0:T(2,128)S(1)} copy-done((f32[4,8,2,129]{3,2,1,0:T(2,128)S(1)}, f32[4,8,2,129]{3,2,1,0:T(2,128)}, u32[]{:S(2)}) %copy-start.3) | copy-done | bytes 33048
  4.3 0.0 copy-start.4
  4.3 0.8 %copy-done.4 = f32[4,8,2,129]{3,2,1,0:T(2,128)S(1)} copy-done((f32[4,8,2,129]{3,2,1,0:T(2,128)S(1)}, f32[4,8,2,129]{3,2,1,0:T(2,128)}, u32[]{:S(2)}) %copy-start.4) | copy-done | bytes 33048
  5.1 0.0 copy-start.5
  5.1 0.7 %copy-done.5 = f32[4,8]{1,0:T(4,128)S(1)} copy-done((f32[4,8]{1,0:T(4,128)S(1)}, f32[4,8]{1,0:T(4,128)}, u32[]{:S(2)}) %copy-start.5) | copy-done | bytes 152
  5.8 0.0 copy-start.6
  5.8 0.7 %copy-done.6 = s32[4]{0:T(128)S(1)} copy-done((s32[4]{0:T(128)S(1)}, s32[4]{0:T(128)}, u32[]{:S(2)}) %copy-start.6) | copy-done | bytes 40
  6.4 0.0 copy-start.7
  6.4 0.7 %copy-done.7 = f32[4]{0:T(128)S(1)} copy-done((f32[4]{0:T(128)S(1)}, f32[4]{0:T(128)}, u32[]{:S(2)}) %copy-start.7) | copy-done | bytes 40
  7.1 43.0 %shard_map.95 = (f32[128,384]{1,0:T(8,128)S(1)}, f32[32,384]{1,0:T(8,128)S(1)}) custom-call(f32[128,384]{1,0:T(8,128)S(1)} %copy-done, s32[128,384]{1,0:T(8,128)S(1)} %copy-done.1, f32[128,384]{1,0:T(8,128)S(1)} %copy-done.2, f32[4,8,2,129]{3,2,1,0:T(2,128)S(1)} %copy-done.3, f32[4,8,2,129]{3,2,1,0:T(2,128)S(1)} %copy-done.4, f32[4,8]{1,0:T(4,128)S(1)} %copy-done.5, ...), custom_call_target="tpu_custom_call" | custom-call | tf_op jit(solution)/shard_map/pallas_call | solution.py:402
  50.1 0.7 %copy.12 = f32[128,384]{1,0:T(8,128)} copy(f32[128,384]{1,0:T(8,128)S(1)} %get-tuple-element.4) | data formatting | bytes 393216
  50.8 0.6 %copy.13 = f32[32,384]{1,0:T(8,128)} copy(f32[32,384]{1,0:T(8,128)S(1)} %get-tuple-element.5) | data formatting | bytes 98304
Async XLA Ops:
  0.6 0.9 %copy-start = (f32[128,384]{1,0:T(8,128)S(1)}, f32[128,384]{1,0:T(8,128)}, u32[]{:S(2)}) copy-start(f32[128,384]{1,0:T(8,128)} %mask_ref.1) | copy-start | bytes 589828
  1.6 0.9 %copy-start.1 = (s32[128,384]{1,0:T(8,128)S(1)}, s32[128,384]{1,0:T(8,128)}, u32[]{:S(2)}) copy-start(s32[128,384]{1,0:T(8,128)} %target_ref.1) | copy-start | bytes 589828
  2.5 0.9 %copy-start.2 = (f32[128,384]{1,0:T(8,128)S(1)}, f32[128,384]{1,0:T(8,128)}, u32[]{:S(2)}) copy-start(f32[128,384]{1,0:T(8,128)} %weight_ref.1) | copy-start | bytes 589828
  3.4 0.8 %copy-start.3 = (f32[4,8,2,129]{3,2,1,0:T(2,128)S(1)}, f32[4,8,2,129]{3,2,1,0:T(2,128)}, u32[]{:S(2)}) copy-start(f32[4,8,2,129]{3,2,1,0:T(2,128)} %rt_ref.1) | copy-start | bytes 99076
  4.3 0.8 %copy-start.4 = (f32[4,8,2,129]{3,2,1,0:T(2,128)S(1)}, f32[4,8,2,129]{3,2,1,0:T(2,128)}, u32[]{:S(2)}) copy-start(f32[4,8,2,129]{3,2,1,0:T(2,128)} %ct_ref.1) | copy-start | bytes 99076
  5.1 0.7 %copy-start.5 = (f32[4,8]{1,0:T(4,128)S(1)}, f32[4,8]{1,0:T(4,128)}, u32[]{:S(2)}) copy-start(f32[4,8]{1,0:T(4,128)} %kw_ref.1) | copy-start | bytes 388
  5.8 0.7 %copy-start.6 = (s32[4]{0:T(128)S(1)}, s32[4]{0:T(128)}, u32[]{:S(2)}) copy-start(s32[4]{0:T(128)} %cs_ref.1) | copy-start | bytes 52
  6.4 0.7 %copy-start.7 = (f32[4]{0:T(128)S(1)}, f32[4]{0:T(128)}, u32[]{:S(2)}) copy-start(f32[4]{0:T(128)} %dose_ref.1) | copy-start | bytes 52

commit v2 on v1

--- a/solution.py
+++ b/solution.py
@@ -18,13 +18,13 @@
 
 
 def kernel(
-    n_t, n_c, mask_ref, target_ref, weight_ref, rt_ref, ct_ref, kw_ref, cs_ref, dose_ref,
+    n_t, n_c, mask_hbm, target_hbm, weight_hbm, rt_hbm, ct_hbm, kw_hbm, cs_hbm, dose_hbm,
     soft_ref, new_ref,
-    xp, xw, tb, ra, cb, cf, fields, ssc, ssend, srecv, infosend, inforecv, fsend, frecv,
+    mask_ref, target_ref, weight_ref, rt_ref, ct_ref, kw_ref, cs_ref, dose_ref, in_s,
+    xp, xw, tb, ra, cb, cbt, cf, fields, ssc, ssend, srecv, infosend, inforecv, fsend, frecv,
     softsend, softrecv, bkr, bkm, rimsend, rimrecv, gown, gsend, grecv, sqsend, sqrecv,
-    sqtsend, sqtrecv,
     halo_s, halo_r, info_s, info_r, s_s, s_r, f_s, f_r, soft_s, soft_r, rim_s, rim_r,
-    g_s, g_r, sq_s, sq_r, sqt_s, sqt_r,
+    g_s, g_r, sq_s, sq_r,
 ):
     t = lax.axis_index("tile")
     z = lax.axis_index("corner")
@@ -54,10 +54,35 @@
         )
 
     barrier = pltpu.get_barrier_semaphore()
-    for d in range(1, n_c):
-        pl.semaphore_signal(barrier, inc=1, device_id=(t, zpeer(d)), device_id_type=MESH)
-    for d in range(1, n_t):
-        pl.semaphore_signal(barrier, inc=1, device_id=(tpeer(d), z), device_id_type=MESH)
+    everyone = n_t * n_c
+
+    def anyone(d):
+        other = lax.rem(t * n_c + z + d, everyone)
+        return (other // n_c, lax.rem(other, n_c))
+
+    def greet(d, _):
+        pl.semaphore_signal(barrier, inc=1, device_id=anyone(d), device_id_type=MESH)
+        return 0
+
+    lax.fori_loop(1, everyone, greet, 0)
+
+    row0 = pl.multiple_of(z * share, share)
+    loads = [
+        pltpu.make_async_copy(src, dst, in_s.at[i])
+        for i, (src, dst) in enumerate([
+            (mask_hbm, mask_ref),
+            (cs_hbm, cs_ref),
+            (dose_hbm, dose_ref),
+            (rt_hbm.at[s_me], rt_ref),
+            (ct_hbm.at[s_me], ct_ref),
+            (kw_hbm, kw_ref),
+            (target_hbm.at[pl.ds(row0, share)], target_ref),
+            (weight_hbm.at[pl.ds(row0, share)], weight_ref),
+        ])
+    ]
+    for load in loads:
+        load.start()
+    loads[0].wait()
 
     padded = jnp.concatenate([mask_ref[...], jnp.zeros((rows, 2 * reach), F32)], axis=1)
     padded = pltpu.roll(padded, reach, 1)
@@ -73,39 +98,22 @@
         xp[reach + rows : ext, :] = jnp.zeros((reach, cols + 2 * reach), BF16)
         rimrecv[0] = jnp.zeros((reach, cols), BF16)
 
+    loads[1].wait()
+    loads[2].wait()
     for i in range(local_corners):
         infosend[2 * i : 2 * i + 1, :] = jnp.full((1, cols), cs_ref[i].astype(F32), F32)
         infosend[2 * i + 1 : 2 * i + 2, :] = jnp.full((1, cols), dose_ref[i], F32)
     inforecv[z] = infosend[...]
 
-    pl.semaphore_wait(barrier, n_c - 1 + n_t - 1)
-
-    down = remote(xp.at[pl.ds(rows, reach)], xp.at[pl.ds(0, reach)],
-                  halo_s.at[0], halo_r.at[0], (tpeer(1), z))
-    up = remote(xp.at[pl.ds(reach, reach)], xp.at[pl.ds(reach + rows, reach)],
-                halo_s.at[1], halo_r.at[1], (tpeer(n_t - 1), z))
-
-    @pl.when(t < n_t - 1)
-    def _():
-        down.start()
-
-    @pl.when(t > 0)
-    def _():
-        up.start()
-
-    infos = [
-        remote(infosend, inforecv.at[z], info_s.at[d - 1], info_r.at[d - 1], (t, zpeer(d)))
-        for d in range(1, n_c)
-    ]
-    for copy in infos:
-        copy.start()
-
     tb[...] = jnp.zeros(tb.shape, F32)
+
+    loads[3].wait()
+    loads[4].wait()
 
     def tables(k, _):
         for p in range(2):
-            tb[p : p + 1, 0:taps] = rt_ref[s_me, k_me + k, p : p + 1, :].astype(BF16).astype(F32)
-            tb[2 + p : 3 + p, 0:taps] = ct_ref[s_me, k_me + k, p : p + 1, :].astype(BF16).astype(F32)
+            tb[p : p + 1, 0:taps] = rt_ref[k_me + k, p : p + 1, :].astype(BF16).astype(F32)
+            tb[2 + p : 3 + p, 0:taps] = ct_ref[k_me + k, p : p + 1, :].astype(BF16).astype(F32)
 
         def band(row, length, width):
             wide = jnp.broadcast_to(tb[row : row + 1, 0:width], (length, width))
@@ -118,36 +126,82 @@
         ra[k, 0:rows, ext : 2 * ext] = (-im).astype(BF16)
         ra[k, rows : 2 * rows, 0:ext] = im.astype(BF16)
         base = pl.multiple_of(k * 2 * BLK, 2 * BLK)
-        cb[pl.ds(base, BLK), :] = band(2, BLK, win).astype(BF16)
-        cb[pl.ds(base + BLK, BLK), :] = band(3, BLK, win).astype(BF16)
+        pair = jnp.concatenate([band(2, BLK, win), band(3, BLK, win)], axis=0)
+        cb[pl.ds(base, 2 * BLK), :] = pair.astype(BF16)
+        cbt[k] = pair.T.astype(BF16)
         return 0
 
     lax.fori_loop(0, per, tables, 0)
 
+    pl.semaphore_wait(barrier, everyone - 1)
+
+    down = remote(xp.at[pl.ds(rows, reach)], xp.at[pl.ds(0, reach)],
+                  halo_s.at[0], halo_r.at[0], (tpeer(1), z))
+    up = remote(xp.at[pl.ds(reach, reach)], xp.at[pl.ds(reach + rows, reach)],
+                halo_s.at[1], halo_r.at[1], (tpeer(n_t - 1), z))
+
+    @pl.when(t < n_t - 1)
+    def _():
+        down.start()
+
     @pl.when(t > 0)
     def _():
-        down.wait_recv()
-
-    @pl.when(t < n_t - 1)
-    def _():
-        up.wait_recv()
+        up.start()
+
+    infos = [
+        remote(infosend, inforecv.at[z], info_s.at[d - 1], info_r.at[d - 1], (t, zpeer(d)))
+        for d in range(1, n_c)
+    ]
+    for copy in infos:
+        copy.start()
 
     for b in range(n_b):
-        xw[b * ext : (b + 1) * ext, :] = xp[:, b * BLK : b * BLK + win]
-    ssc[...] = jnp.zeros(ssc.shape, F32)
-
-    def forward(k, _):
-        base = pl.multiple_of(k * 2 * BLK, 2 * BLK)
-        c = lax.dot_general(
-            xw[...], cb[pl.ds(base, 2 * BLK), :], (((1,), (1,)), ((), ())),
-            preferred_element_type=F32,
-        ).astype(BF16)
+        xw[b * rows : (b + 1) * rows, :] = xp[reach : reach + rows, b * BLK : b * BLK + win]
+
+    def middle_columns(k, _):
+        c = jnp.dot(xw[0 : n_b * rows, :], cbt[k], preferred_element_type=F32).astype(BF16)
         for b in range(n_b):
             for p in range(2):
-                cf[p * ext : (p + 1) * ext, b * BLK : (b + 1) * BLK] = c[
-                    b * ext : (b + 1) * ext, p * BLK : (p + 1) * BLK
+                low = p * ext + reach
+                cf[k, low : low + rows, b * BLK : (b + 1) * BLK] = c[
+                    b * rows : (b + 1) * rows, p * BLK : (p + 1) * BLK
                 ]
-        field = jnp.dot(ra[k], cf[...], preferred_element_type=F32)
+        return 0
+
+    lax.fori_loop(0, per, middle_columns, 0)
+
+    @pl.when(t > 0)
+    def _():
+        down.wait_recv()
+
+    @pl.when(t < n_t - 1)
+    def _():
+        up.wait_recv()
+
+    side = n_b * rows
+    for b in range(n_b):
+        low = side + b * 2 * reach
+        cut = slice(b * BLK, b * BLK + win)
+        xw[low : low + reach, :] = xp[0:reach, cut]
+        xw[low + reach : low + 2 * reach, :] = xp[reach + rows : ext, cut]
+    ssc[...] = jnp.zeros(ssc.shape, F32)
+    for load in loads[5:]:
+        load.wait()
+
+    def rim_columns(k, _):
+        c = jnp.dot(xw[side:, :], cbt[k], preferred_element_type=F32).astype(BF16)
+        for b in range(n_b):
+            for p in range(2):
+                piece = c[b * 2 * reach : (b + 1) * 2 * reach, p * BLK : (p + 1) * BLK]
+                out = slice(b * BLK, (b + 1) * BLK)
+                cf[k, p * ext : p * ext + reach, out] = piece[0:reach]
+                cf[k, p * ext + reach + rows : (p + 1) * ext, out] = piece[reach:]
+        return 0
+
+    lax.fori_loop(0, per, rim_columns, 0)
+
+    def forward(k, _):
+        field = jnp.dot(ra[k], cf[k], preferred_element_type=F32)
         re = field[0:rows]
         im = field[rows : 2 * rows]
         power = kw_ref[s_me, k_me + k] * (re * re + im * im)
@@ -170,7 +224,6 @@
     for copy in scopies:
         copy.wait_recv()
 
-    row0 = pl.multiple_of(z * share, share)
     owners = n_c // n_sets
     step = 16
 
@@ -182,8 +235,8 @@
             for o in range(1, owners):
                 total = total + srecv[s * owners + o, pl.ds(r, step), :].astype(F32)
             sums.append(total)
-        goal = target_ref[pl.ds(row0 + r, step), :].astype(F32)
-        pixel = weight_ref[pl.ds(row0 + r, step), :]
+        goal = target_ref[pl.ds(r, step), :].astype(F32)
+        pixel = weight_ref[pl.ds(r, step), :]
         for b in range(n_b):
             cut = slice(b * BLK, (b + 1) * BLK)
             den = jnp.zeros((step, BLK), F32)
@@ -223,12 +276,12 @@
         remote(softsend, softrecv.at[z], soft_s.at[d - 1], soft_r.at[d - 1], (t, zpeer(d)))
         for d in range(1, n_c)
     ]
-    for copy in softs:
-        copy.start()
     frecv[z] = fsend[s_me]
     softrecv[z] = softsend[...]
     for copy in fcopies:
         copy.wait_recv()
+    for copy in softs:
+        copy.start()
 
     def backward(k, _):
         factor = frecv[...].reshape(rows, cols).astype(F32) * kw_ref[s_me, k_me + k]
@@ -310,27 +363,23 @@
     part = square[:, 0:BLK]
     for b in range(1, n_b):
         part = part + square[:, b * BLK : (b + 1) * BLK]
-    sqsend[...] = part
-    sqz = [
-        remote(sqsend, sqrecv.at[d - 1], sq_s.at[d - 1], sq_r.at[d - 1], (t, zpeer(d)))
-        for d in range(1, n_c)
-    ]
-    for copy in sqz:
-        copy.start()
-    for d in range(1, n_c):
-        sqz[d - 1].wait_recv()
-        part = part + sqrecv[d - 1]
-    sqtsend[...] = part
-    sqt = [
-        remote(sqtsend, sqtrecv.at[d - 1], sqt_s.at[d - 1], sqt_r.at[d - 1], (tpeer(d), z))
-        for d in range(1, n_t)
-    ]
-    for copy in sqt:
-        copy.start()
-    for d in range(1, n_t):
-        sqt[d - 1].wait_recv()
-        part = part + sqtrecv[d - 1]
-    total = jnp.sum(jnp.sum(part, axis=0, keepdims=True), axis=1, keepdims=True)
+    sqsend[...] = jnp.sum(part, axis=0, keepdims=True)
+
+    def square_copy(d):
+        return remote(sqsend, sqrecv.at[d - 1], sq_s.at[d - 1], sq_r.at[d - 1], anyone(d))
+
+    def square_start(d, _):
+        square_copy(d).start()
+        return 0
+
+    def square_wait(d, _):
+        square_copy(d).wait_recv()
+        return 0
+
+    lax.fori_loop(1, everyone, square_start, 0)
+    lax.fori_loop(1, everyone, square_wait, 0)
+    part = sqsend[...] + jnp.sum(sqrecv[...], axis=0)
+    total = jnp.sum(part, axis=1, keepdims=True)
     rate = step_rate / jnp.sqrt(total / (rows * n_t * cols) + small_eps)
     own = mask_ref[pl.ds(row0, share), :]
     new_ref[...] = jnp.clip(own - rate * grad, 0.0, 1.0)
@@ -345,8 +394,14 @@
         up.wait_send()
         rim_up.wait_send()
 
-    for copy in infos + scopies + fcopies + softs + gcopies + sqz + sqt:
+    for copy in infos + scopies + fcopies + softs + gcopies:
         copy.wait_send()
+
+    def square_sent(d, _):
+        square_copy(d).wait_send()
+        return 0
+
+    lax.fori_loop(1, everyone, square_sent, 0)
 
 
 def solution(mesh):
@@ -361,17 +416,28 @@
         per = n_sets * n_k // n_c
         info_rows = 8 * ((2 * corner_set.shape[0] + 7) // 8)
         vmem = pl.BlockSpec(memory_space=pltpu.VMEM)
-        smem = pl.BlockSpec(memory_space=pltpu.SMEM)
+        hbm = pl.BlockSpec(memory_space=pl.ANY)
+        S = pltpu.SMEM
         V = pltpu.VMEM
         dma = pltpu.SemaphoreType.DMA
         zc = dma((n_c - 1,))
         scratch = [
+            V((rows, cols), F32),
+            V((share, cols), jnp.int32),
+            V((share, cols), F32),
+            V((n_k, 2, taps), F32),
+            V((n_k, 2, taps), F32),
+            S((n_sets, n_k), F32),
+            S(corner_set.shape, jnp.int32),
+            S(dose.shape, F32),
+            dma((8,)),
             V((ext, cols + 2 * reach), BF16),
             V((n_b * ext, win), BF16),
             V((8, max(ext, win)), F32),
             V((per, 2 * rows, 2 * ext), BF16),
             V((per * 2 * BLK, win), BF16),
-            V((2 * ext, cols), BF16),
+            V((per, win, 2 * BLK), BF16),
+            V((per, 2 * ext, cols), BF16),
             V((per, 2 * rows, cols), BF16),
             V((n_c, share, cols), F32),
             V((n_c, share, cols), BF16),
@@ -389,15 +455,13 @@
             V((n_c, share, cols), F32),
             V((n_c, share, cols), BF16),
             V((n_c - 1, share, cols), BF16),
-            V((8, BLK), F32),
-            V((n_c - 1, 8, BLK), F32),
-            V((8, BLK), F32),
-            V((n_t - 1, 8, BLK), F32),
+            V((1, BLK), F32),
+            V((n_t * n_c - 1, 1, BLK), F32),
             dma((2,)), dma((2,)),
             zc, zc, zc, zc, zc, zc, zc, zc,
             dma((2,)), dma((2,)),
-            zc, zc, zc, zc,
-            dma((n_t - 1,)), dma((n_t - 1,)),
+            zc, zc,
+            dma((n_t * n_c - 1,)), dma((n_t * n_c - 1,)),
         ]
         return pl.pallas_call(
             functools.partial(kernel, n_t, n_c),
@@ -405,11 +469,11 @@
                 jax.ShapeDtypeStruct((rows, cols), F32),
                 jax.ShapeDtypeStruct((share, cols), F32),
             ),
-            in_specs=[vmem] * 5 + [smem] * 3,
+            in_specs=[hbm] * 8,
             out_specs=(vmem, vmem),
             scratch_shapes=scratch,
             compiler_params=pltpu.CompilerParams(
-                collective_id=0, has_side_effects=True, vmem_limit_bytes=44 * 1024 * 1024
+                collective_id=0, has_side_effects=True, vmem_limit_bytes=60 * 1024 * 1024
             ),
         )(mask, target, pixel_weight, row_taps, col_taps, kernel_weights, corner_set, dose)
 

time: 51.7 us -> 43.8 us (0.85)
  local copies, waits for them, and re-layouts: 7.74 us -> 2.25 us
  Pallas kernels: 43 us -> 40.8 us
    unnamed x18 -> x4, local copies, waits for them, and re-layouts: 7.74 us -> 2.25 us
    pallas_call x1, Pallas kernels: 43 us -> 40.8 us  [local(): pl.pallas_call(functools.partial(kernel, n_t, n_c), out_shape=(jax.ShapeD...]
where the time goes in v2:
time: 43.8 us; the launch traced here: 43.7 us
  Pallas kernels  40.8 us (93%)
  local copies, waits for them, and re-layouts  2.25 us (5%)
  between operations  0.65 us (1%)
    pallas_call x1, Pallas kernels, local(): pl.pallas_call(functools.partial(kernel, n_t, n_c), out_shape=(jax.ShapeD...  40.8 us
    unnamed x4, local copies, waits for them, and re-layouts  2.25 us

profile of v2, /device:TPU:0, one launch (start us, length us, event | category | flops | bytes accessed | tf_op | source)
XLA Modules:
  0.0 43.7 jit_solution(6966617513669593596)
XLA Ops:
  0.6 40.8 %shard_map.95 = (f32[128,384]{1,0:T(8,128)}, f32[32,384]{1,0:T(8,128)}) custom-call(f32[128,384]{1,0:T(8,128)} %mask_hbm.1, s32[128,384]{1,0:T(8,128)} %target_hbm.1, f32[128,384]{1,0:T(8,128)} %weight_hbm.1, f32[4,8,2,129]{3,2,1,0:T(2,128)} %rt_hbm.1, f32[4,8,2,129]{3,2,1,0:T(2,128)} %ct_hbm.1, f32[4,8]{1,0:T(4,128)} %kw_hbm.1, s32[4]{0:T(128)} %cs_hbm.1, ...), custom_call_target="tpu_custom_call" | custom-call | tf_op jit(solution)/shard_map/pallas_call | solution.py:466
  41.4 0.0 copy-start
  41.4 1.6 %copy.12 = f32[128,384]{1,0:T(8,128)} copy(f32[128,384]{1,0:T(8,128)} %get-tuple-element.4) | data formatting | bytes 393216
  43.1 0.0 copy-done
  43.1 0.6 %copy.13 = f32[32,384]{1,0:T(8,128)} copy(f32[32,384]{1,0:T(8,128)S(1)} %copy-done) | data formatting | bytes 98304
Async XLA Ops:
  41.4 1.6 %copy-start = (f32[32,384]{1,0:T(8,128)S(1)}, f32[32,384]{1,0:T(8,128)}, u32[]{:S(2)}) copy-start(f32[32,384]{1,0:T(8,128)} %get-tuple-element.5) | copy-start | bytes 147460

commit v3 on v2

--- a/solution.py
+++ b/solution.py
@@ -64,7 +64,7 @@
         pl.semaphore_signal(barrier, inc=1, device_id=anyone(d), device_id_type=MESH)
         return 0
 
-    lax.fori_loop(1, everyone, greet, 0)
+    lax.fori_loop(1, everyone, greet, 0, unroll=4)
 
     row0 = pl.multiple_of(z * share, share)
     loads = [
@@ -168,7 +168,7 @@
                 ]
         return 0
 
-    lax.fori_loop(0, per, middle_columns, 0)
+    lax.fori_loop(0, per, middle_columns, 0, unroll=True)
 
     @pl.when(t > 0)
     def _():
@@ -198,7 +198,7 @@
                 cf[k, p * ext + reach + rows : (p + 1) * ext, out] = piece[reach:]
         return 0
 
-    lax.fori_loop(0, per, rim_columns, 0)
+    lax.fori_loop(0, per, rim_columns, 0, unroll=True)
 
     def forward(k, _):
         field = jnp.dot(ra[k], cf[k], preferred_element_type=F32)
@@ -209,7 +209,7 @@
         fields[k] = field.astype(BF16)
         return 0
 
-    lax.fori_loop(0, per, forward, 0)
+    lax.fori_loop(0, per, forward, 0, unroll=True)
 
     ssend[...] = ssc[...].astype(BF16)
     scopies = [
@@ -300,7 +300,7 @@
                 bkm[b * rows : (b + 1) * rows, at] = piece[reach : reach + rows]
         return 0
 
-    lax.fori_loop(0, per, backward, 0)
+    lax.fori_loop(0, per, backward, 0, unroll=True)
 
     def column_sum(ref, count):
         g = jnp.dot(ref[...], cb[...], preferred_element_type=F32)
@@ -376,8 +376,8 @@
         square_copy(d).wait_recv()
         return 0
 
-    lax.fori_loop(1, everyone, square_start, 0)
-    lax.fori_loop(1, everyone, square_wait, 0)
+    lax.fori_loop(1, everyone, square_start, 0, unroll=4)
+    lax.fori_loop(1, everyone, square_wait, 0, unroll=4)
     part = sqsend[...] + jnp.sum(sqrecv[...], axis=0)
     total = jnp.sum(part, axis=1, keepdims=True)
     rate = step_rate / jnp.sqrt(total / (rows * n_t * cols) + small_eps)
@@ -401,7 +401,7 @@
         square_copy(d).wait_send()
         return 0
 
-    lax.fori_loop(1, everyone, square_sent, 0)
+    lax.fori_loop(1, everyone, square_sent, 0, unroll=4)
 
 
 def solution(mesh):

time: 43.8 us -> 39.2 us (0.89)
  Pallas kernels: 40.8 us -> 36.2 us
    pallas_call x1, Pallas kernels: 40.8 us -> 36.2 us  [local(): pl.pallas_call(functools.partial(kernel, n_t, n_c), out_shape=(jax.ShapeD...]
where the time goes in v3:
time: 39.2 us; the launch traced here: 39.1 us
  Pallas kernels  36.2 us (92%)
  local copies, waits for them, and re-layouts  2.25 us (6%)
  between operations  0.65 us (2%)
    pallas_call x1, Pallas kernels, local(): pl.pallas_call(functools.partial(kernel, n_t, n_c), out_shape=(jax.ShapeD...  36.2 us
    unnamed x4, local copies, waits for them, and re-layouts  2.25 us

profile of v3, /device:TPU:0, one launch (start us, length us, event | category | flops | bytes accessed | tf_op | source)
XLA Modules:
  0.0 39.1 jit_solution(10328033197808514513)
XLA Ops:
  0.6 36.2 %shard_map.95 = (f32[128,384]{1,0:T(8,128)}, f32[32,384]{1,0:T(8,128)}) custom-call(f32[128,384]{1,0:T(8,128)} %mask_hbm.1, s32[128,384]{1,0:T(8,128)} %target_hbm.1, f32[128,384]{1,0:T(8,128)} %weight_hbm.1, f32[4,8,2,129]{3,2,1,0:T(2,128)} %rt_hbm.1, f32[4,8,2,129]{3,2,1,0:T(2,128)} %ct_hbm.1, f32[4,8]{1,0:T(4,128)} %kw_hbm.1, s32[4]{0:T(128)} %cs_hbm.1, ...), custom_call_target="tpu_custom_call" | custom-call | tf_op jit(solution)/shard_map/pallas_call | solution.py:466
  36.8 0.0 copy-start
  36.8 1.6 %copy.12 = f32[128,384]{1,0:T(8,128)} copy(f32[128,384]{1,0:T(8,128)} %get-tuple-element.4) | data formatting | bytes 393216
  38.5 0.0 copy-done
  38.5 0.6 %copy.13 = f32[32,384]{1,0:T(8,128)} copy(f32[32,384]{1,0:T(8,128)S(1)} %copy-done) | data formatting | bytes 98304
Async XLA Ops:
  36.8 1.6 %copy-start = (f32[32,384]{1,0:T(8,128)S(1)}, f32[32,384]{1,0:T(8,128)}, u32[]{:S(2)}) copy-start(f32[32,384]{1,0:T(8,128)} %get-tuple-element.5) | copy-start | bytes 147460
